TPU v7x, 128 devices: a whole 4x4x4 slice. The times are simulated.
128 devices in a mesh: row: 16 (over z_hi, x, core), col: 8 (over z_lo, y).
Axes of the slice: x: 4, y: 4, z: 4 (z_hi: 2, z_lo: 2; z = z_hi * 2 + z_lo), core: 2. Of those that a mesh axis runs over, the one named last changes fastest.
Arguments:
- momentum: bfloat16 [6144, 8192], P('row', 'col'), may hold values from -0.029831067 to 0.029831067
Outputs:
- update: bfloat16 [6144, 8192], P('row', 'col')
All inputs are finite; a program needn't handle non-finite values.
Results may differ from a plain program's by a relative error of at most 0.0035.
Values may be sent and summed in bfloat16 or wider, within the bound.
A program may use at most 128 MiB of HBM per device.

v0:
```python
import math

import jax
import jax.numpy as jnp
from jax import lax
from jax.sharding import PartitionSpec as P

M = 6144
N = 8192


def shards(momentum):
    column_rows = lax.all_gather(momentum, "row", axis=0, tiled=True)
    partial_value = lax.dot_general(
        momentum, column_rows, (((1,), (1,)), ((), ())), preferred_element_type=jnp.float32
    )
    gram_block = lax.psum_scatter(partial_value, "col", scatter_dimension=1, tiled=True).astype(
        jnp.bfloat16
    )
    gram_full = lax.all_gather(gram_block, "col", axis=1, tiled=True)
    square = jnp.dot(
        gram_full,
        lax.all_gather(gram_block, "row", axis=0, tiled=True),
        preferred_element_type=jnp.float32,
    )
    mixed = (-4.775 * gram_block.astype(jnp.float32) + 2.0315 * square).astype(jnp.bfloat16)
    mixed_full = lax.all_gather(mixed, "col", axis=1, tiled=True)
    result = 3.4445 * momentum.astype(jnp.float32) + jnp.dot(
        mixed_full, column_rows, preferred_element_type=jnp.float32
    )
    factor = 0.2 * math.sqrt(max(M, N))
    return (factor * result).astype(jnp.bfloat16)


def solution(mesh):
    placed = (P("row", "col"),)
    return jax.shard_map(
        shards, mesh=mesh, in_specs=placed, out_specs=P("row", "col"), check_vma=False
    )
```

profile of v0, /device:TPU:1, one launch (start us, length us, event | category | flops | bytes accessed | tf_op | source)
XLA Modules:
  0.0 438.5 jit_solution(5118839298306835027)
XLA Ops:
  6.5 0.0 all-gather.5.cloned.1.call-start
  6.5 0.7 all-gather.5.cloned.1.call-update
  7.3 0.0 reduce-scatter.2.cloned.1.call-start
  7.3 97.1 %all-gather.5.cloned.1.call-done = bf16[6144,1024]{1,0:T(8,128)(2,1)} async-done(((bf16[384,1024]{1,0:T(8,128)(2,1)}), bf16[6144,1024]{1,0:T(8,128)(2,1)}) %all-gather.5.cloned.1.call-update) | async-done | bytes 12582928 | tf_op jit(solution)/shard_map/all_gather | solution.py:13
  104.4 15.4 %fusion.2 = f32[384,6144]{1,0:T(8,128)} fusion(bf16[384,1024]{1,0:T(8,128)(2,1)} %param.1, bf16[6144,1024]{1,0:T(8,128)(2,1)} %all-gather.5.cloned.1.call-done), kind=kOutput, calls=%fused_computation.4 | convolution fusion | flops 4831838208 | bytes 22806528 | tf_op jit(solution)/shard_map/dot_general | solution.py:14
  119.8 0.0 reduce-scatter.2.cloned.1.call-update
  119.9 0.0 all-gather.7.cloned.1.call-start
  119.9 100.0 %reduce-scatter.2.cloned.1.call-done = f32[384,768]{1,0:T(8,128)} async-done(((f32[384,6144]{1,0:T(8,128)}), f32[384,768]{1,0:T(8,128)}) %reduce-scatter.2.cloned.1.call-update) | async-done | bytes 1179664 | tf_op jit(solution)/shard_map/reduce_scatter | solution.py:17
  219.9 2.1 convert_element_type.16
  222.1 0.0 all-gather.7.cloned.1.call-update
  222.1 0.0 all-gather.9.cloned.1.call-start
  222.1 0.5 all-gather.9.cloned.1.call-update
  222.7 0.0 copy-start
  222.7 0.0 all-gather.11.cloned.1.call-start
  222.7 55.8 %all-gather.7.cloned.1.call-done = bf16[384,6144]{1,0:T(8,128)(2,1)} async-done(((bf16[384,768]{1,0:T(8,128)(2,1)}), bf16[384,6144]{1,0:T(8,128)(2,1)}) %all-gather.7.cloned.1.call-update) | async-done | bytes 4718608 | tf_op jit(solution)/shard_map/all_gather | solution.py:20
  278.5 78.6 %all-gather.9.cloned.1.call-done = bf16[6144,768]{1,0:T(8,128)(2,1)} async-done(((bf16[384,768]{1,0:T(8,128)(2,1)}), bf16[6144,768]{1,0:T(8,128)(2,1)}) %all-gather.9.cloned.1.call-update) | async-done | bytes 9437200 | tf_op jit(solution)/shard_map/all_gather | solution.py:23
  357.1 9.7 %fusion.1 = bf16[384,768]{1,0:T(8,128)(2,1)} fusion(bf16[384,6144]{1,0:T(8,128)(2,1)} %all-gather.7.cloned.1.call-done, bf16[6144,768]{1,0:T(8,128)(2,1)} %all-gather.9.cloned.1.call-done, bf16[384,768]{1,0:T(8,128)(2,1)} %convert_element_type.16), kind=kOutput, calls=%fused_computation.3 | convolution fusion | flops 3625353216 | bytes 15335424 | tf_op jit(solution)/shard_map/dot_general | solution.py:21
  366.8 0.0 all-gather.11.cloned.1.call-update
  366.8 55.0 %all-gather.11.cloned.1.call-done = bf16[384,6144]{1,0:T(8,128)(2,1)} async-done(((bf16[384,768]{1,0:T(8,128)(2,1)}), bf16[384,6144]{1,0:T(8,128)(2,1)}) %all-gather.11.cloned.1.call-update) | async-done | bytes 4718608 | tf_op jit(solution)/shard_map/all_gather | solution.py:27
  421.8 0.0 copy-done
  421.8 10.1 %multiply_convert_fusion = bf16[384,1024]{1,0:T(8,128)(2,1)} fusion(bf16[384,1024]{1,0:T(8,128)(2,1)S(1)} %copy-done, bf16[384,6144]{1,0:T(8,128)(2,1)} %all-gather.11.cloned.1.call-done, bf16[6144,1024]{1,0:T(8,128)(2,1)} %all-gather.5.cloned.1.call-done), kind=kOutput, calls=%fused_computation | convolution fusion | flops 4833804288 | bytes 18874368 | tf_op jit(solution)/shard_map/dot_general | solution.py:28
Async XLA Ops:
  6.5 97.9 %all-gather.5.cloned.1.call-start = ((), (), s32[]{:S(2)}) async-start(), calls=%async_computation.1 | async-start | bytes 13369344 | tf_op jit(solution)/shard_map/all_gather | solution.py:13
  7.3 212.7 %reduce-scatter.2.cloned.1.call-start = ((), (), s32[]{:S(2)}) async-start(), calls=%async_computation.2 | async-start | bytes 10616832 | tf_op jit(solution)/shard_map/reduce_scatter | solution.py:17
  119.9 158.7 %all-gather.7.cloned.1.call-start = ((), (), s32[]{:S(2)}) async-start(), calls=%async_computation.3 | async-start | bytes 5308416 | tf_op jit(solution)/shard_map/all_gather | solution.py:20
  222.1 135.0 %all-gather.9.cloned.1.call-start = ((), (), s32[]{:S(2)}) async-start(), calls=%async_computation.4 | async-start | bytes 10027008 | tf_op jit(solution)/shard_map/all_gather | solution.py:23
  222.7 199.1 %copy-start = (bf16[384,1024]{1,0:T(8,128)(2,1)S(1)}, bf16[384,1024]{1,0:T(8,128)(2,1)}, u32[]{:S(2)}) copy-start(bf16[384,1024]{1,0:T(8,128)(2,1)} %param.1) | copy-start | bytes 2359300
  222.7 199.1 %all-gather.11.cloned.1.call-start = ((), (), s32[]{:S(2)}) async-start(), calls=%async_computation.5 | async-start | bytes 5308416 | tf_op jit(solution)/shard_map/all_gather | solution.py:27
Sparse Core Ops, SparseCore 0:
  9.8 94.5 all-gather.4
  120.0 99.8 reduce-scatter.1
  222.2 56.2 all-gather.6
  280.8 76.2 all-gather.8
  367.0 54.8 all-gather.10
where the time goes:
time: 439 us; the launch traced here: 438 us
  waiting for transfers between devices  388 us (88%)
  matrix products  35.3 us (8%)
  between operations  13.1 us (3%)
    reduce_scatter x1, waiting for transfers between devices, shards(): lax.psum_scatter(partial_value, 'col', scatter_dimension=1, tiled=True)  100 us
    all_gather x1, waiting for transfers between devices, shards(): column_rows = lax.all_gather(momentum, 'row', axis=0, tiled=True)  97.1 us
    all_gather x1, waiting for transfers between devices, shards(): lax.all_gather(gram_block, 'row', axis=0, tiled=True)  78.6 us
    all_gather x1, waiting for transfers between devices, shards(): gram_full = lax.all_gather(gram_block, 'col', axis=1, tiled=True)  55.8 us
    all_gather x1, waiting for transfers between devices, shards(): mixed_full = lax.all_gather(mixed, 'col', axis=1, tiled=True)  55 us
    dot_general x1, matrix products, shards(): lax.dot_general(momentum, column_rows, (((1,), (1,)), ((), ())), preferre...  15.4 us
    dot_general x1, matrix products, shards(): jnp.dot(mixed_full, column_rows, preferred_element_type=jnp.float32)  10.1 us
    dot_general x1, matrix products, shards(): jnp.dot(gram_full, lax.all_gather(gram_block, 'row', axis=0, tiled=True),...  9.72 us
  transfers between devices with their start and end apart: 5, of which 5 were waited for; matrix products, arithmetic and copies ran while one was open for 0% of the time, Pallas kernels for 0%

commit v1 on v0

v1 whole, which is shorter than its diff:
```python
import functools
import math

import jax
import jax.numpy as jnp
from jax import lax
from jax.experimental import pallas as pl
from jax.experimental.pallas import tpu as pltpu
from jax.sharding import PartitionSpec as P

M = 6144
N = 8192
MESH = pl.DeviceIdType.MESH
BF = jnp.bfloat16
F32 = jnp.float32

A, B, C = 3.4445, -4.775, 2.0315
FACTOR = 0.2 * math.sqrt(max(M, N))

R = 384
S_ROWS = 2 * R
K = 1024
Q = R // 4
H = Q // 2
N_SITES = 240


def kernel(x_ref, o_ref, xc, wc, pb, g, r1l, r1r, r2l, r2r, zr, ua, local_sem, send_sem, recv_sem):
    row = lax.axis_index("row")
    col = lax.axis_index("col")
    zh, x, core = row // 8, (row % 8) // 2, row % 2
    zl, y = col // 4, col % 4

    xr = {"row": zh * 8 + ((x + 1) % 4) * 2 + core}
    xl = {"row": zh * 8 + ((x + 3) % 4) * 2 + core}
    zp = {"row": (1 - zh) * 8 + x * 2 + core}
    sib = {"row": zh * 8 + x * 2 + (1 - core)}
    yr = {"col": zl * 4 + (y + 1) % 4}
    yl = {"col": zl * 4 + (y + 3) % 4}
    zq = {"col": (1 - zl) * 4 + y}

    def block(dz, dx):
        return ((zh + dz) % 2) * 4 + (x + dx) % 4

    own_copy = pltpu.make_async_copy(x_ref, xc.at[block(0, 0), pl.ds(core * R, R)], local_sem)
    own_copy.start()

    barrier = pltpu.get_barrier_semaphore()
    for peer in (xr, xl, zp, sib, yr, yl, zq):
        pl.semaphore_signal(barrier, inc=1, device_id=peer, device_id_type=MESH)
    pl.semaphore_wait(barrier, 7)

    sites = {}
    pending = []

    def site(name):
        return sites.setdefault(name, len(sites))

    def send(name, src, dst, device):
        i = site(name)
        copy = pltpu.make_async_remote_copy(
            src_ref=src, dst_ref=dst, send_sem=send_sem.at[i], recv_sem=recv_sem.at[i],
            device_id=device, device_id_type=MESH,
        )
        copy.start()
        pending.append(copy)

    def recv(name, view):
        i = site(name)
        pltpu.make_async_remote_copy(
            src_ref=view, dst_ref=view, send_sem=send_sem.at[i], recv_sem=recv_sem.at[i],
            device_id=sib, device_id_type=MESH,
        ).wait_recv()

    def ag(tag, buf, off, n):
        h = n // 2

        def at(dz, dx, o=0, m=n, c=core):
            return buf.at[block(dz, dx), pl.ds(pl.multiple_of(c * R + off + o, 16), m)]

        def to(name, dz, dx, device, o=0, m=n, src=None):
            send(tag + name, at(dz, dx, o, m) if src is None else src, at(dz, dx, o, m), device)

        def own(src=None):
            to("own_r", 0, 0, xr, src=src)
            to("own_l", 0, 0, xl, src=src)
            to("own_z", 0, 0, zp, src=src)
            to("own_s", 0, 0, sib, src=src)

        def near():
            recv(tag + "own_z", at(1, 0))
            to("z_r", 1, 0, xr)
            to("z_l", 1, 0, xl)
            to("z_s", 1, 0, sib)
            recv(tag + "own_r", at(0, -1))
            to("own_rr", 0, -1, xr, 0, h)
            to("l_s", 0, -1, sib)
            recv(tag + "own_l", at(0, 1))
            to("own_ll", 0, 1, xl, h, h)
            to("r_s", 0, 1, sib)

        def mid():
            recv(tag + "z_r", at(1, -1))
            to("z_rr", 1, -1, xr, 0, h)
            to("zl_s", 1, -1, sib)
            recv(tag + "z_l", at(1, 1))
            to("z_ll", 1, 1, xl, h, h)
            to("zr_s", 1, 1, sib)

        def far():
            recv(tag + "own_rr", at(0, 2, 0, h))
            to("f1_s", 0, 2, sib, 0, h)
            recv(tag + "own_ll", at(0, 2, h, h))
            to("f2_s", 0, 2, sib, h, h)

        def last():
            recv(tag + "z_rr", at(1, 2, 0, h))
            to("zf1_s", 1, 2, sib, 0, h)
            recv(tag + "z_ll", at(1, 2, h, h))
            to("zf2_s", 1, 2, sib, h, h)

        def from_sib(dz, dx):
            other = 1 - core
            if dx == 2:
                names = ("zf1_s", "zf2_s") if dz else ("f1_s", "f2_s")
                recv(tag + names[0], at(dz, dx, 0, h, other))
                recv(tag + names[1], at(dz, dx, h, h, other))
                return
            name = {(0, 0): "own_s", (0, -1): "l_s", (0, 1): "r_s", (1, 0): "z_s", (1, -1): "zl_s", (1, 1): "zr_s"}
            recv(tag + name[dz, dx], at(dz, dx, 0, n, other))

        return own, near, mid, far, last, from_sib

    q0, qr, ql, q2 = y * Q, ((y + 1) % 4) * Q, ((y + 3) % 4) * Q, ((y + 2) % 4) * Q

    def rows(off, n):
        return pl.ds(pl.multiple_of(off, 16), n)

    nt = (((1,), (1,)), ((), ()))

    def partial_gram(s):
        for n in range(S_ROWS // 256):
            cols = slice(n * 256, n * 256 + 256)
            p = lax.dot_general(x_ref[...], xc[s, cols, :], nt, preferred_element_type=F32)
            pb[s, :, cols] = p.astype(BF)

    def add(s, off, n, other):
        here = (s, rows(off, n), slice(None))
        pb[here] = (pb[here].astype(F32) + other.astype(F32)).astype(BF)

    def rs1(i, s):
        send(f"rs1r{i}", pb.at[s, rows(q2, H)], r1l.at[s], yr)
        send(f"rs1l{i}", pb.at[s, rows(q2 + H, H)], r1r.at[s], yl)

    def rs2(i, s):
        recv(f"rs1r{i}", r1l.at[s])
        add(s, qr, H, r1l[s])
        send(f"rs2r{i}", pb.at[s, rows(qr, Q)], r2l.at[s], yr)
        recv(f"rs1l{i}", r1r.at[s])
        add(s, ql + H, H, r1r[s])
        send(f"rs2l{i}", pb.at[s, rows(ql, Q)], r2r.at[s], yl)

    def rs3(i, s):
        recv(f"rs2r{i}", r2l.at[s])
        recv(f"rs2l{i}", r2r.at[s])
        add(s, q0, Q, r2l[s].astype(F32) + r2r[s].astype(F32))
        send(f"rs3{i}", pb.at[s, rows(q0, Q)], zr.at[s], zq)

    def rs4(i, s):
        recv(f"rs3{i}", zr.at[s])
        here = (s, rows(q0, Q), slice(None))
        g[here] = (pb[here].astype(F32) + zr[s].astype(F32)).astype(BF)
        send(f"g_r{i}", g.at[s, rows(q0, Q)], g.at[s, rows(q0, Q)], yr)
        send(f"g_l{i}", g.at[s, rows(q0, Q)], g.at[s, rows(q0, Q)], yl)

    def gag(i, s):
        recv(f"g_r{i}", g.at[s, rows(ql, Q)])
        send(f"g_rr{i}", g.at[s, rows(ql, H)], g.at[s, rows(ql, H)], yr)
        recv(f"g_l{i}", g.at[s, rows(qr, Q)])
        send(f"g_ll{i}", g.at[s, rows(qr + H, H)], g.at[s, rows(qr + H, H)], yl)

    def gag_far(i, s):
        recv(f"g_rr{i}", g.at[s, rows(q2, H)])
        recv(f"g_ll{i}", g.at[s, rows(q2 + H, H)])

    own, near, mid, far, last, from_sib = ag("x", xc, 0, R)
    own(x_ref)
    own_copy.wait()

    order = [(0, 0), (1, 0), (0, -1), (0, 1), (1, -1), (1, 1), (0, 2), (1, 2)]
    ids = [block(*d) for d in order]
    stage = [partial_gram, rs1, rs2, rs3, rs4]

    def reduce_steps(i, upto=8):
        if 0 <= i - 1 < 8:
            rs2(i - 1, ids[i - 1])
        if 0 <= i - 2 < 8:
            rs3(i - 2, ids[i - 2])
        if 0 <= i - 3 < 8:
            rs4(i - 3, ids[i - 3])

    events = {1: near, 4: mid, 6: far, 7: last}
    for i, d in enumerate(order):
        if i in events:
            events[i]()
        from_sib(*d)
        partial_gram(ids[i])
        rs1(i, ids[i])
        reduce_steps(i)
    for i in range(8, 11):
        reduce_steps(i)

    def weights(offs):
        for n in range(K // 256):
            cols = slice(n * 256, n * 256 + 256)

            def body(s, acc):
                lhs = [g[s, rows(off, Q), :] for off in offs]
                lhs = lhs[0] if len(lhs) == 1 else jnp.concatenate(lhs, axis=0)
                return acc + jnp.dot(lhs, xc[s, :, cols], preferred_element_type=F32)

            acc = lax.fori_loop(0, 8, body, jnp.zeros((Q * len(offs), 256), F32))
            for j, off in enumerate(offs):
                w = B * x_ref[rows(off, Q), cols].astype(F32) + C * acc[j * Q : (j + 1) * Q]
                wc[block(0, 0), rows(core * R + off, Q), cols] = w.astype(BF)

    quarters = [ag(f"w{j}", wc, off, Q) for j, off in enumerate((q0, ql, qr, q2))]

    weights([q0])
    quarters[0][0]()
    for i in range(8):
        gag(i, ids[i])
    quarters[0][1]()
    weights([ql, qr])
    quarters[1][0]()
    quarters[2][0]()
    quarters[0][2]()
    quarters[0][3]()
    for i in range(8):
        gag_far(i, ids[i])
    weights([q2])
    quarters[3][0]()
    quarters[0][4]()
    for j in (1, 2):
        quarters[j][1]()
    for j in (1, 2):
        quarters[j][2]()
        quarters[j][3]()
    quarters[3][1]()
    for j in (1, 2):
        quarters[j][4]()

    def update(first, s):
        for n in range(K // 256):
            cols = slice(n * 256, n * 256 + 256)
            u = jnp.dot(g[s], wc[s, :, cols], preferred_element_type=F32)
            ua[:, cols] = A * x_ref[:, cols].astype(F32) + u if first else ua[:, cols] + u

    def gathered(d):
        for quarter in quarters:
            quarter[5](*d)

    for i, d in enumerate(order):
        if i == 4:
            quarters[3][2]()
            quarters[3][3]()
        if i == 7:
            quarters[3][4]()
        gathered(d)
        update(i == 0, ids[i])
    o_ref[...] = (FACTOR * ua[...]).astype(BF)

    for copy in pending:
        copy.wait_send()
    assert len(sites) <= N_SITES


def shards(momentum):
    vmem = pl.BlockSpec(memory_space=pltpu.VMEM)
    return pl.pallas_call(
        kernel,
        out_shape=jax.ShapeDtypeStruct((R, K), BF),
        in_specs=[vmem],
        out_specs=vmem,
        scratch_shapes=[
            pltpu.VMEM((8, S_ROWS, K), BF),
            pltpu.VMEM((8, S_ROWS, K), BF),
            pltpu.VMEM((8, R, S_ROWS), BF),
            pltpu.VMEM((8, R, S_ROWS), BF),
            pltpu.VMEM((8, H, S_ROWS), BF),
            pltpu.VMEM((8, H, S_ROWS), BF),
            pltpu.VMEM((8, Q, S_ROWS), BF),
            pltpu.VMEM((8, Q, S_ROWS), BF),
            pltpu.VMEM((8, Q, S_ROWS), BF),
            pltpu.VMEM((R, K), F32),
            pltpu.SemaphoreType.DMA,
            pltpu.SemaphoreType.DMA((N_SITES,)),
            pltpu.SemaphoreType.DMA((N_SITES,)),
        ],
        compiler_params=pltpu.CompilerParams(
            collective_id=0, has_side_effects=True, vmem_limit_bytes=58 << 20
        ),
        cost_estimate=pl.CostEstimate(flops=15 * 10**9, bytes_accessed=2 * R * K * 2, transcendentals=0),
    )(momentum)


def solution(mesh):
    placed = (P("row", "col"),)
    return jax.shard_map(
        shards, mesh=mesh, in_specs=placed, out_specs=P("row", "col"), check_vma=False
    )
```

time: 439 us -> 166 us (0.38)
  waiting for transfers between devices: 388 us -> 0 us
  Pallas kernels: 0 us -> 164 us
  matrix products: 35.3 us -> 0 us
  between operations: 13.1 us -> 0.01 us
    all_gather x4 -> x0, waiting for transfers between devices: 286 us -> none  [the longest x1 97.1 us: shards(): column_rows = lax.all_gather(momentum, 'row', axis=0, tiled=True)]
    pallas_call x0 -> x1, Pallas kernels: none -> 164 us  [shards(): pl.pallas_call(kernel, out_shape=jax.ShapeDtypeStruct((R, K), BF), in_spe...]
    reduce_scatter x1 -> x0, waiting for transfers between devices: 100 us -> none  [shards(): lax.psum_scatter(partial_value, 'col', scatter_dimension=1, tiled=True)]
    dot_general x3 -> x0, matrix products: 35.3 us -> none  [the longest x1 15.4 us: shards(): lax.dot_general(momentum, column_rows, (((1,), (1,)), ((), ())), preferre...]
  transfers between devices with their start and end apart: 5 -> 0, of which waited for: 5 -> 0; matrix products, arithmetic and copies ran while one was open for 0% -> 0% of each run, Pallas kernels for 0% -> 0%
where the time goes in v1:
time: 166 us
  Pallas kernels  164 us (99%)
  local copies, waits for them, and re-layouts  2.06 us (1%)
    pallas_call x1, Pallas kernels, shards(): pl.pallas_call(kernel, out_shape=jax.ShapeDtypeStruct((R, K), BF), in_spe...  164 us

profile of v1, /device:TPU:1, one launch (start us, length us, event | category | flops | bytes accessed | tf_op | source)
XLA Modules:
  0.0 165.9 jit_solution(9915714653014005026)
XLA Ops:
  0.0 163.9 %shard_map.17 = bf16[384,1024]{1,0:T(8,128)(2,1)} custom-call(bf16[384,1024]{1,0:T(8,128)(2,1)} %x_ref.1), custom_call_target="tpu_custom_call" | custom-call | flops 15000000512 | bytes 1572864 | tf_op jit(solution)/shard_map/pallas_call | solution.py:280
  163.9 2.1 %copy.3 = bf16[384,1024]{1,0:T(8,128)(2,1)} copy(bf16[384,1024]{1,0:T(8,128)(2,1)} %shard_map.17) | data formatting | bytes 1572864

commit v2 on v0

v2 whole, which is shorter than its diff:
```python
import functools
import math

import jax
import jax.numpy as jnp
from jax import lax
from jax.experimental import pallas as pl
from jax.experimental.pallas import tpu as pltpu
from jax.sharding import PartitionSpec as P

M = 6144
N = 8192
MESH = pl.DeviceIdType.MESH
BF = jnp.bfloat16
F32 = jnp.float32

A, B, C = 3.4445, -4.775, 2.0315
FACTOR = 0.2 * math.sqrt(max(M, N))

R = 384
S_ROWS = 2 * R
K = 1024
Q = R // 4
H = Q // 2

ORDER = [(0, 0), (0, 3), (0, 1), (1, 0), (0, 2), (1, 2), (1, 3), (1, 1)]
SHAPE = (8, 2, 2, 2, 2, H, K)
HALF = R
N_SEND = 56
N_RECV = 188
CUT = 5


def slot(dz, dx):
    return ORDER.index((dz % 2, dx % 4))


def kernel(x_hbm, o_ref, x_ref, xc, wc, pb, g, r1l, r1r, r2l, r2r, zr, yb, ua, local_sem, send_sem, recv_sem):
    row = lax.axis_index("row")
    col = lax.axis_index("col")
    zh, x, core = row // 8, (row % 8) // 2, row % 2
    zl, y = col // 4, col % 4

    peers = {
        "xr": {"row": zh * 8 + ((x + 1) % 4) * 2 + core},
        "xl": {"row": zh * 8 + ((x + 3) % 4) * 2 + core},
        "zp": {"row": (1 - zh) * 8 + x * 2 + core},
        "sib": {"row": zh * 8 + x * 2 + (1 - core)},
        "yr": {"col": zl * 4 + (y + 1) % 4},
        "yl": {"col": zl * 4 + (y + 3) % 4},
        "zq": {"col": (1 - zl) * 4 + y},
    }

    own_copy = pltpu.make_async_copy(x_hbm, x_ref, local_sem.at[0])
    own_copy.start()
    barrier = pltpu.get_barrier_semaphore()
    for peer in peers.values():
        pl.semaphore_signal(barrier, inc=1, device_id=peer, device_id_type=MESH)
    own_copy.wait()
    places = [
        pltpu.make_async_copy(x_ref.at[pl.ds((c * 4 + i) * H, H)], xc.at[0, c, core, i // 2, i % 2], local_sem.at[1 + c * 4 + i])
        for c in range(2) for i in range(4)
    ]
    for place in places:
        place.start()
    for place in places:
        place.wait()
    pl.semaphore_wait(barrier, len(peers))

    sites = {}
    pending = []

    def site(name):
        return sites.setdefault(name, len(sites))

    def send(name, src, dst, peer):
        i = site(name)
        n = len(pending)
        if n >= N_SEND:
            pending[n - N_SEND].wait_send()
        copy = pltpu.make_async_remote_copy(
            src_ref=src, dst_ref=dst, send_sem=send_sem.at[n % N_SEND], recv_sem=recv_sem.at[i],
            device_id=peers[peer], device_id_type=MESH,
        )
        copy.start()
        pending.append(copy)

    def recv(name, view):
        i = site(name)
        pltpu.make_async_remote_copy(
            src_ref=view, dst_ref=view, send_sem=send_sem.at[0], recv_sem=recv_sem.at[i],
            device_id=peers["sib"], device_id_type=MESH,
        ).wait_recv()

    def rows(off, n):
        return pl.ds(pl.multiple_of(off, 16), n)

    class Gather:
        def __init__(self, tag, buf, index):
            self.tag, self.buf, self.index = tag, buf, index

        def at(self, dz, dx, part=None, c=core):
            view = self.buf.at[(slot(dz, dx), *self.index(c))]
            return view if part is None else view.at[part]

        def to(self, name, dz, dx, peer, part=None):
            there = {"xr": (dz, dx - 1), "xl": (dz, dx + 1), "zp": (1 - dz, dx), "sib": (dz, dx)}[peer]
            send(self.tag + name, self.at(dz, dx, part), self.at(*there, part), peer)

        def recv(self, name, dz, dx, part=None, c=core):
            recv(self.tag + name, self.at(dz, dx, part, c))

        def own(self):
            self.to("own_r", 0, 0, "xr")
            self.to("own_l", 0, 0, "xl")
            self.to("own_z", 0, 0, "zp")
            self.to("own_s", 0, 0, "sib")

        def near(self):
            self.recv("own_r", 0, -1)
            self.to("own_rr", 0, -1, "xr", 0)
            self.to("l_s", 0, -1, "sib")
            self.recv("own_l", 0, 1)
            self.to("own_ll", 0, 1, "xl", 1)
            self.to("r_s", 0, 1, "sib")

        def near_z(self):
            self.recv("own_z", 1, 0)
            self.to("z_s", 1, 0, "sib")

        def pass_z(self):
            self.to("z_r", 1, 0, "xr")
            self.to("z_l", 1, 0, "xl")

        def far(self):
            self.recv("own_rr", 0, 2, 0)
            self.recv("own_ll", 0, 2, 1)
            self.to("f_z", 0, 2, "zp")
            self.to("f_s", 0, 2, "sib")

        def far_z(self):
            self.recv("f_z", 1, 2)
            self.to("zf_s", 1, 2, "sib")

        def mid(self):
            self.recv("z_r", 1, -1)
            self.to("zl_s", 1, -1, "sib")
            self.recv("z_l", 1, 1)
            self.to("zr_s", 1, 1, "sib")

        def from_sib(self, i):
            name = ["own_s", "l_s", "r_s", "z_s", "f_s", "zf_s", "zl_s", "zr_s"][i]
            self.recv(name, *ORDER[i], None, 1 - core)

    q0, qr, ql, q2 = y * Q, ((y + 1) % 4) * Q, ((y + 3) % 4) * Q, ((y + 2) % 4) * Q
    nt = (((1,), (1,)), ((), ()))

    def partial_gram(s, c):
        block = xc[s, c].reshape(HALF, K)
        for m in range(2):
            mine = slice(m * R // 2, (m + 1) * R // 2)
            p = lax.dot_general(x_ref[mine, :], block, nt, preferred_element_type=F32)
            pb[s, c, mine, :] = p.astype(BF)

    def add(s, c, off, n, other):
        here = (s, c, rows(off, n), slice(None))
        pb[here] = (pb[here].astype(F32) + other.astype(F32)).astype(BF)

    def begin(s, c):
        gx[c].from_sib(s)
        partial_gram(s, c)
        send(f"rs1r{s}{c}", pb.at[s, c, rows(q2, H)], r1l.at[s, c], "yr")
        send(f"rs1l{s}{c}", pb.at[s, c, rows(q2 + H, H)], r1r.at[s, c], "yl")

    def rs2(s, c):
        recv(f"rs1r{s}{c}", r1l.at[s, c])
        add(s, c, qr, H, r1l[s, c])
        send(f"rs2r{s}{c}", pb.at[s, c, rows(qr, Q)], r2l.at[s, c], "yr")
        recv(f"rs1l{s}{c}", r1r.at[s, c])
        add(s, c, ql + H, H, r1r[s, c])
        send(f"rs2l{s}{c}", pb.at[s, c, rows(ql, Q)], r2r.at[s, c], "yl")

    def rs3(s, c):
        recv(f"rs2r{s}{c}", r2l.at[s, c])
        recv(f"rs2l{s}{c}", r2r.at[s, c])
        add(s, c, q0, Q, r2l[s, c].astype(F32) + r2r[s, c].astype(F32))
        send(f"rs3{s}{c}", pb.at[s, c, rows(q0, Q)], zr.at[s, c], "zq")

    def rs4(s, c):
        recv(f"rs3{s}{c}", zr.at[s, c])
        total = pb[s, c, rows(q0, Q), :].astype(F32) + zr[s, c].astype(F32)
        g[s, rows(q0, Q), c * HALF : (c + 1) * HALF] = total.astype(BF)

    class GatherGram:
        def __init__(self, s0, s1):
            self.s0, self.s1 = s0, s1

        def at(self, off, t):
            return g.at[self.s0 : self.s1, rows(off + t * H, H)]

        def own(self, t):
            send(f"g_r{self.s0}{t}", self.at(q0, t), self.at(q0, t), "yr")
            send(f"g_l{self.s0}{t}", self.at(q0, t), self.at(q0, t), "yl")

        def near(self, t):
            recv(f"g_r{self.s0}{t}", self.at(ql, t))
            recv(f"g_l{self.s0}{t}", self.at(qr, t))
            if t == 0:
                send(f"g_rr{self.s0}", self.at(ql, 0), self.at(ql, 0), "yr")
            else:
                send(f"g_ll{self.s0}", self.at(qr, 1), self.at(qr, 1), "yl")

        def far(self):
            recv(f"g_rr{self.s0}", self.at(q2, 0))
            recv(f"g_ll{self.s0}", self.at(q2, 1))

    def product(offs, places, s0, s1):
        for n in range(K // 256):
            cols = slice(n * 256, n * 256 + 256)
            part = None
            for s in range(s0, s1):
                lhs = jnp.concatenate([g[s, rows(off, H), :] for off in offs], axis=0)
                rhs = xc[s, :, :, :, :, :, cols].reshape(S_ROWS, 256)
                d = jnp.dot(lhs, rhs, preferred_element_type=F32)
                part = d if part is None else part + d
            for j, (off, place) in enumerate(zip(offs, places)):
                p = part[j * H : (j + 1) * H]
                if s0 > 0:
                    p += yb[rows(off, H), cols]
                if s1 < 8:
                    yb[rows(off, H), cols] = p
                else:
                    w = B * x_ref[rows(off, H), cols].astype(F32) + C * p
                    wc[(0, *place, slice(None), cols)] = w.astype(BF)

    def update(s):
        for n in range(K // 256):
            cols = slice(n * 256, n * 256 + 256)
            u = jnp.dot(g[s], wc[s, :, :, :, :, :, cols].reshape(S_ROWS, 256), preferred_element_type=F32)
            u += ua[:, cols] if s > 0 else A * x_ref[:, cols].astype(F32)
            if s < 7:
                ua[:, cols] = u
            else:
                o_ref[:, cols] = (FACTOR * u).astype(BF)

    hi, lo = y // 2, y % 2
    gx = [Gather(f"x{c}", xc, lambda k, c=c: (c, k)) for c in range(2)]
    gw = [
        Gather("w0", wc, lambda k: (hi, k, lo)),
        Gather("w1", wc, lambda k: (slice(None), k, 1 - lo, 0)),
        Gather("w2", wc, lambda k: (slice(None), k, 1 - lo, 1)),
        Gather("w3", wc, lambda k: (1 - hi, k, lo)),
    ]
    even, odd = (1 - lo) * Q, (3 - lo) * Q
    w0 = ([q0, q0 + H], [(hi, core, lo, 0), (hi, core, lo, 1)])
    w1 = ([even, odd], [(0, core, 1 - lo, 0), (1, core, 1 - lo, 0)])
    w2 = ([even + H, odd + H], [(0, core, 1 - lo, 1), (1, core, 1 - lo, 1)])
    w3 = ([q2, q2 + H], [(1 - hi, core, lo, 0), (1 - hi, core, lo, 1)])
    g1, g2 = GatherGram(0, CUT), GatherGram(CUT, 8)

    def each(f, units):
        for u in units:
            f(*u)

    gx[0].own()
    gx[1].own()
    each(begin, [(0, 0), (0, 1)])
    each(rs2, [(0, 0), (0, 1)])
    gx[0].near()
    gx[0].near_z()
    each(begin, [(1, 0), (2, 0), (3, 0)])
    each(rs3, [(0, 0), (0, 1)])
    each(rs2, [(1, 0), (2, 0)])
    gx[1].near()
    gx[0].pass_z()
    gx[1].near_z()
    gx[1].pass_z()
    each(begin, [(1, 1), (2, 1), (3, 1)])
    each(rs2, [(3, 0)])
    gx[0].far()
    each(begin, [(4, 0)])
    each(rs4, [(0, 0), (0, 1)])
    each(rs2, [(1, 1), (2, 1)])
    each(rs3, [(1, 0), (2, 0), (3, 0)])
    gx[1].far()
    each(begin, [(4, 1)])
    each(rs2, [(3, 1), (4, 0)])
    each(rs3, [(1, 1), (2, 1)])
    each(rs4, [(1, 0), (2, 0), (3, 0)])
    each(rs2, [(4, 1)])
    each(rs3, [(3, 1), (4, 0)])
    gx[0].far_z()
    each(begin, [(5, 0)])
    gx[0].mid()
    each(begin, [(6, 0), (7, 0)])
    each(rs3, [(4, 1)])
    each(rs2, [(5, 0)])
    each(rs4, [(1, 1), (2, 1), (3, 1), (4, 0)])
    each(rs2, [(6, 0), (7, 0)])
    each(rs3, [(5, 0)])
    gx[1].far_z()
    each(begin, [(5, 1)])
    gx[1].mid()
    each(begin, [(6, 1), (7, 1)])
    each(rs2, [(5, 1)])
    each(rs3, [(6, 0), (7, 0)])
    each(rs2, [(6, 1), (7, 1)])
    each(rs4, [(4, 1)])
    g1.own(0)
    product(*w0, 0, CUT)
    each(rs3, [(5, 1)])
    each(rs4, [(5, 0), (6, 0), (7, 0)])
    each(rs3, [(6, 1), (7, 1)])
    each(rs4, [(5, 1), (6, 1), (7, 1)])
    g2.own(0)
    g1.own(1)
    g2.own(1)
    product(*w0, CUT, 8)
    gw[0].own()
    g1.near(0)
    g2.near(0)
    gw[0].near()
    gw[0].near_z()
    gw[0].pass_z()
    product(*w1, 0, 8)
    gw[1].own()
    gw[0].far()
    gw[1].near()
    gw[1].near_z()
    gw[1].pass_z()
    gw[0].far_z()
    gw[0].mid()
    g1.near(1)
    g2.near(1)
    product(*w2, 0, 8)
    gw[2].own()
    gw[1].far()
    gw[2].near()
    gw[2].near_z()
    gw[2].pass_z()
    gw[1].far_z()
    gw[1].mid()
    g1.far()
    g2.far()
    product(*w3, 0, 8)
    gw[3].own()
    gw[2].far()
    gw[3].near()
    gw[3].near_z()
    gw[3].pass_z()
    gw[2].far_z()
    gw[2].mid()
    gw[3].far()

    def end(s):
        for part in gw:
            part.from_sib(s)
        update(s)

    for s in range(5):
        end(s)
    gw[3].far_z()
    gw[3].mid()
    for s in range(5, 8):
        end(s)

    for copy in pending[-N_SEND:]:
        copy.wait_send()
    assert len(sites) == N_RECV, len(sites)


def shards(momentum):
    unit = (8, 2, Q, HALF)
    return pl.pallas_call(
        kernel,
        out_shape=jax.ShapeDtypeStruct((R, K), BF),
        in_specs=[pl.BlockSpec(memory_space=pl.ANY)],
        out_specs=pl.BlockSpec(memory_space=pltpu.VMEM),
        scratch_shapes=[
            pltpu.VMEM((R, K), BF),
            pltpu.VMEM(SHAPE, BF),
            pltpu.VMEM(SHAPE, BF),
            pltpu.VMEM((8, 2, R, HALF), BF),
            pltpu.VMEM((8, R, S_ROWS), BF),
            pltpu.VMEM((8, 2, H, HALF), BF),
            pltpu.VMEM((8, 2, H, HALF), BF),
            pltpu.VMEM(unit, BF),
            pltpu.VMEM(unit, BF),
            pltpu.VMEM(unit, BF),
            pltpu.VMEM((R, K), F32),
            pltpu.VMEM((R, K), F32),
            pltpu.SemaphoreType.DMA((9,)),
            pltpu.SemaphoreType.DMA((N_SEND,)),
            pltpu.SemaphoreType.DMA((N_RECV,)),
        ],
        compiler_params=pltpu.CompilerParams(
            collective_id=0, has_side_effects=True, vmem_limit_bytes=58 << 20
        ),
        cost_estimate=pl.CostEstimate(flops=15 * 10**9, bytes_accessed=2 * R * K * 2, transcendentals=0),
    )(momentum)


def solution(mesh):
    placed = (P("row", "col"),)
    return jax.shard_map(
        shards, mesh=mesh, in_specs=placed, out_specs=P("row", "col"), check_vma=False
    )
```

time: 439 us -> 141 us (0.32)
  waiting for transfers between devices: 388 us -> 0 us
  Pallas kernels: 0 us -> 138 us
  matrix products: 35.3 us -> 0 us
  between operations: 13.1 us -> 0.01 us
    all_gather x4 -> x0, waiting for transfers between devices: 286 us -> none  [the longest x1 97.1 us: shards(): column_rows = lax.all_gather(momentum, 'row', axis=0, tiled=True)]
    pallas_call x0 -> x1, Pallas kernels: none -> 138 us  [shards(): pl.pallas_call(kernel, out_shape=jax.ShapeDtypeStruct((R, K), BF), in_spe...]
    reduce_scatter x1 -> x0, waiting for transfers between devices: 100 us -> none  [shards(): lax.psum_scatter(partial_value, 'col', scatter_dimension=1, tiled=True)]
    dot_general x3 -> x0, matrix products: 35.3 us -> none  [the longest x1 15.4 us: shards(): lax.dot_general(momentum, column_rows, (((1,), (1,)), ((), ())), preferre...]
  transfers between devices with their start and end apart: 5 -> 0, of which waited for: 5 -> 0; matrix products, arithmetic and copies ran while one was open for 0% -> 0% of each run, Pallas kernels for 0% -> 0%
where the time goes in v2:
time: 141 us
  Pallas kernels  138 us (98%)
  local copies, waits for them, and re-layouts  2.06 us (1%)
    pallas_call x1, Pallas kernels, shards(): pl.pallas_call(kernel, out_shape=jax.ShapeDtypeStruct((R, K), BF), in_spe...  138 us

profile of v2, /device:TPU:1, one launch (start us, length us, event | category | flops | bytes accessed | tf_op | source)
XLA Modules:
  0.0 140.5 jit_solution(6391183638988170311)
XLA Ops:
  0.0 138.4 %shard_map.17 = bf16[384,1024]{1,0:T(8,128)(2,1)} custom-call(bf16[384,1024]{1,0:T(8,128)(2,1)} %x_hbm.1), custom_call_target="tpu_custom_call" | custom-call | flops 15000000512 | bytes 1572864 | tf_op jit(solution)/shard_map/pallas_call | solution.py:374
  138.5 2.1 %copy.3 = bf16[384,1024]{1,0:T(8,128)(2,1)} copy(bf16[384,1024]{1,0:T(8,128)(2,1)} %shard_map.17) | data formatting | bytes 1572864

commit v3 on v2

--- a/solution.py
+++ b/solution.py
@@ -27,8 +27,8 @@
 SHAPE = (8, 2, 2, 2, 2, H, K)
 HALF = R
 N_SEND = 56
-N_RECV = 188
-CUT = 5
+N_RECV = 194
+GROUPS = [(0, 2), (2, 5), (5, 8)]
 
 
 def slot(dz, dx):
@@ -237,8 +237,8 @@
         for n in range(K // 256):
             cols = slice(n * 256, n * 256 + 256)
             u = jnp.dot(g[s], wc[s, :, :, :, :, :, cols].reshape(S_ROWS, 256), preferred_element_type=F32)
-            u += ua[:, cols] if s > 0 else A * x_ref[:, cols].astype(F32)
-            if s < 7:
+            u += ua[:, cols] if s != 1 else A * x_ref[:, cols].astype(F32)
+            if s != 5:
                 ua[:, cols] = u
             else:
                 o_ref[:, cols] = (FACTOR * u).astype(BF)
@@ -256,113 +256,144 @@
     w1 = ([even, odd], [(0, core, 1 - lo, 0), (1, core, 1 - lo, 0)])
     w2 = ([even + H, odd + H], [(0, core, 1 - lo, 1), (1, core, 1 - lo, 1)])
     w3 = ([q2, q2 + H], [(1 - hi, core, lo, 0), (1 - hi, core, lo, 1)])
-    g1, g2 = GatherGram(0, CUT), GatherGram(CUT, 8)
+    gg = [GatherGram(s0, s1) for s0, s1 in GROUPS]
 
     def each(f, units):
         for u in units:
             f(*u)
-
-    gx[0].own()
-    gx[1].own()
-    each(begin, [(0, 0), (0, 1)])
-    each(rs2, [(0, 0), (0, 1)])
-    gx[0].near()
-    gx[0].near_z()
-    each(begin, [(1, 0), (2, 0), (3, 0)])
-    each(rs3, [(0, 0), (0, 1)])
-    each(rs2, [(1, 0), (2, 0)])
-    gx[1].near()
-    gx[0].pass_z()
-    gx[1].near_z()
-    gx[1].pass_z()
-    each(begin, [(1, 1), (2, 1), (3, 1)])
-    each(rs2, [(3, 0)])
-    gx[0].far()
-    each(begin, [(4, 0)])
-    each(rs4, [(0, 0), (0, 1)])
-    each(rs2, [(1, 1), (2, 1)])
-    each(rs3, [(1, 0), (2, 0), (3, 0)])
-    gx[1].far()
-    each(begin, [(4, 1)])
-    each(rs2, [(3, 1), (4, 0)])
-    each(rs3, [(1, 1), (2, 1)])
-    each(rs4, [(1, 0), (2, 0), (3, 0)])
-    each(rs2, [(4, 1)])
-    each(rs3, [(3, 1), (4, 0)])
-    gx[0].far_z()
-    each(begin, [(5, 0)])
-    gx[0].mid()
-    each(begin, [(6, 0), (7, 0)])
-    each(rs3, [(4, 1)])
-    each(rs2, [(5, 0)])
-    each(rs4, [(1, 1), (2, 1), (3, 1), (4, 0)])
-    each(rs2, [(6, 0), (7, 0)])
-    each(rs3, [(5, 0)])
-    gx[1].far_z()
-    each(begin, [(5, 1)])
-    gx[1].mid()
-    each(begin, [(6, 1), (7, 1)])
-    each(rs2, [(5, 1)])
-    each(rs3, [(6, 0), (7, 0)])
-    each(rs2, [(6, 1), (7, 1)])
-    each(rs4, [(4, 1)])
-    g1.own(0)
-    product(*w0, 0, CUT)
-    each(rs3, [(5, 1)])
-    each(rs4, [(5, 0), (6, 0), (7, 0)])
-    each(rs3, [(6, 1), (7, 1)])
-    each(rs4, [(5, 1), (6, 1), (7, 1)])
-    g2.own(0)
-    g1.own(1)
-    g2.own(1)
-    product(*w0, CUT, 8)
-    gw[0].own()
-    g1.near(0)
-    g2.near(0)
-    gw[0].near()
-    gw[0].near_z()
-    gw[0].pass_z()
-    product(*w1, 0, 8)
-    gw[1].own()
-    gw[0].far()
-    gw[1].near()
-    gw[1].near_z()
-    gw[1].pass_z()
-    gw[0].far_z()
-    gw[0].mid()
-    g1.near(1)
-    g2.near(1)
-    product(*w2, 0, 8)
-    gw[2].own()
-    gw[1].far()
-    gw[2].near()
-    gw[2].near_z()
-    gw[2].pass_z()
-    gw[1].far_z()
-    gw[1].mid()
-    g1.far()
-    g2.far()
-    product(*w3, 0, 8)
-    gw[3].own()
-    gw[2].far()
-    gw[3].near()
-    gw[3].near_z()
-    gw[3].pass_z()
-    gw[2].far_z()
-    gw[2].mid()
-    gw[3].far()
 
     def end(s):
         for part in gw:
             part.from_sib(s)
         update(s)
 
-    for s in range(5):
-        end(s)
+    gx[0].own()
+    gx[1].own()
+    each(begin, [(0, 1), (0, 0)])
+    each(rs2, [(0, 0)])
+    gx[0].near()
+    gx[0].near_z()
+    each(begin, [(2, 0), (1, 0)])
+    each(rs2, [(0, 1)])
+    each(rs3, [(0, 0)])
+    each(rs2, [(1, 0)])
+    each(begin, [(3, 0)])
+    each(rs3, [(0, 1)])
+    each(rs2, [(2, 0)])
+    gx[1].near()
+    each(begin, [(1, 1)])
+    each(rs3, [(1, 0)])
+    gx[1].near_z()
+    each(rs2, [(3, 0)])
+    each(begin, [(2, 1)])
+    gx[0].far()
+    each(begin, [(3, 1)])
+    each(rs4, [(0, 0)])
+    gx[0].pass_z()
+    each(rs2, [(1, 1)])
+    each(begin, [(4, 0)])
+    each(rs2, [(3, 1)])
+    gx[1].far()
+    each(begin, [(4, 1)])
+    each(rs3, [(1, 1)])
+    each(rs4, [(0, 1)])
+    each(rs2, [(4, 0), (2, 1)])
+    each(rs3, [(3, 0)])
+    each(rs2, [(4, 1)])
+    gx[1].pass_z()
+    gx[0].far_z()
+    gx[0].mid()
+    each(begin, [(7, 0), (6, 0)])
+    each(rs3, [(2, 1)])
+    each(begin, [(5, 0)])
+    each(rs2, [(7, 0), (5, 0)])
+    each(rs3, [(2, 0)])
+    each(rs2, [(6, 0)])
+    gx[1].far_z()
+    gx[1].mid()
+    each(rs4, [(1, 0), (1, 1)])
+    each(rs3, [(4, 0)])
+    each(begin, [(5, 1)])
+    each(rs3, [(3, 1)])
+    each(begin, [(6, 1)])
+    gg[0].own(0)
+    each(begin, [(7, 1)])
+    each(rs4, [(2, 0), (2, 1)])
+    each(rs3, [(4, 1), (5, 0)])
+    each(rs2, [(5, 1), (6, 1)])
+    product(*w0, 0, 2)
+    each(rs2, [(7, 1)])
+    each(rs3, [(7, 0)])
+    each(rs4, [(4, 0), (3, 1)])
+    each(rs3, [(5, 1)])
+    each(rs4, [(3, 0)])
+    gg[0].own(1)
+    each(rs3, [(6, 1)])
+    each(rs4, [(4, 1)])
+    gg[1].own(1)
+    gg[1].own(0)
+    each(rs4, [(5, 0)])
+    each(rs3, [(7, 1)])
+    product(*w0, 2, 5)
+    each(rs4, [(6, 1), (7, 0)])
+    each(rs3, [(6, 0)])
+    each(rs4, [(7, 1), (5, 1), (6, 0)])
+    gg[2].own(0)
+    gg[2].own(1)
+    product(*w0, 5, 8)
+    gw[0].own()
+    gg[0].near(0)
+    gg[0].near(1)
+    gg[1].near(1)
+    product(*w2, 0, 5)
+    gw[0].near()
+    product(*w1, 0, 2)
+    gw[0].near_z()
+    gg[1].near(0)
+    product(*w1, 2, 5)
+    gw[0].pass_z()
+    gg[2].near(0)
+    product(*w1, 5, 8)
+    gw[1].own()
+    gw[0].mid()
+    gg[2].near(1)
+    product(*w2, 5, 8)
+    gw[2].own()
+    gw[0].far()
+    gw[1].near()
+    gg[0].far()
+    product(*w3, 0, 2)
+    gw[1].near_z()
+    gw[1].pass_z()
+    gg[1].far()
+    product(*w3, 2, 5)
+    gw[2].near_z()
+    gw[2].near()
+    gw[1].far()
+    gg[2].far()
+    product(*w3, 5, 8)
+    gw[3].own()
+    gw[2].far()
+    gw[1].far_z()
+    gw[2].pass_z()
+    gw[0].far_z()
+    gw[3].near()
+    gw[3].near_z()
+    gw[3].pass_z()
+    end(1)
+    end(0)
+    end(2)
+    gw[3].far()
+    gw[2].far_z()
+    gw[1].mid()
+    end(3)
+    end(4)
+    gw[2].mid()
+    gw[3].mid()
+    end(6)
     gw[3].far_z()
-    gw[3].mid()
-    for s in range(5, 8):
-        end(s)
+    end(7)
+    end(5)
 
     for copy in pending[-N_SEND:]:
         copy.wait_send()

time: 141 us -> 130 us (0.922)
  Pallas kernels: 138 us -> 128 us
    pallas_call x1, Pallas kernels: 138 us -> 128 us  [shards(): pl.pallas_call(kernel, out_shape=jax.ShapeDtypeStruct((R, K), BF), in_spe...]
where the time goes in v3:
time: 130 us
  Pallas kernels  128 us (98%)
  local copies, waits for them, and re-layouts  2.06 us (2%)
    pallas_call x1, Pallas kernels, shards(): pl.pallas_call(kernel, out_shape=jax.ShapeDtypeStruct((R, K), BF), in_spe...  128 us

profile of v3, /device:TPU:1, one launch (start us, length us, event | category | flops | bytes accessed | tf_op | source)
XLA Modules:
  0.0 130.0 jit_solution(6491199843106332886)
XLA Ops:
  0.0 127.9 %shard_map.17 = bf16[384,1024]{1,0:T(8,128)(2,1)} custom-call(bf16[384,1024]{1,0:T(8,128)(2,1)} %x_hbm.1), custom_call_target="tpu_custom_call" | custom-call | flops 15000000512 | bytes 1572864 | tf_op jit(solution)/shard_map/pallas_call | solution.py:405
  127.9 2.1 %copy.3 = bf16[384,1024]{1,0:T(8,128)(2,1)} copy(bf16[384,1024]{1,0:T(8,128)(2,1)} %shard_map.17) | data formatting | bytes 1572864

commit v4 on v3

--- a/solution.py
+++ b/solution.py
@@ -27,7 +27,8 @@
 SHAPE = (8, 2, 2, 2, 2, H, K)
 HALF = R
 N_SEND = 56
-N_RECV = 194
+N_RECV = 182
+MODES = {"x0": "B", "x1": "B", "w0": "B", "w1": "C", "w2": "B", "w3": "A"}
 GROUPS = [(0, 2), (2, 5), (5, 8)]
 
 
@@ -51,20 +52,17 @@
         "zq": {"col": (1 - zl) * 4 + y},
     }
 
-    own_copy = pltpu.make_async_copy(x_hbm, x_ref, local_sem.at[0])
-    own_copy.start()
+    copies = [pltpu.make_async_copy(x_hbm, x_ref, local_sem.at[0])]
+    for i in range(8):
+        place = xc.at[0, i // 4, core, i // 2 % 2, i % 2]
+        copies.append(pltpu.make_async_copy(x_hbm.at[pl.ds(i * H, H)], place, local_sem.at[1 + i]))
+    for copy in copies:
+        copy.start()
     barrier = pltpu.get_barrier_semaphore()
     for peer in peers.values():
         pl.semaphore_signal(barrier, inc=1, device_id=peer, device_id_type=MESH)
-    own_copy.wait()
-    places = [
-        pltpu.make_async_copy(x_ref.at[pl.ds((c * 4 + i) * H, H)], xc.at[0, c, core, i // 2, i % 2], local_sem.at[1 + c * 4 + i])
-        for c in range(2) for i in range(4)
-    ]
-    for place in places:
-        place.start()
-    for place in places:
-        place.wait()
+    for copy in copies:
+        copy.wait()
     pl.semaphore_wait(barrier, len(peers))
 
     sites = {}
@@ -97,7 +95,8 @@
 
     class Gather:
         def __init__(self, tag, buf, index):
-            self.tag, self.buf, self.index = tag, buf, index
+            self.tag, self.buf, self.index, self.seen = tag, buf, index, set()
+            self.mode = MODES[tag]
 
         def at(self, dz, dx, part=None, c=core):
             view = self.buf.at[(slot(dz, dx), *self.index(c))]
@@ -119,38 +118,70 @@
         def near(self):
             self.recv("own_r", 0, -1)
             self.to("own_rr", 0, -1, "xr", 0)
-            self.to("l_s", 0, -1, "sib")
             self.recv("own_l", 0, 1)
             self.to("own_ll", 0, 1, "xl", 1)
-            self.to("r_s", 0, 1, "sib")
+            self.both("lr_s", 1)
+            if self.mode == "C":
+                send(self.tag + "lr_z", self.pair(1, core), self.pair(6, core), "zp")
+            if self.mode == "H":
+                send(self.tag + "lr_z", self.pair(1, core, 1), self.pair(6, core, 1), "zp")
 
         def near_z(self):
             self.recv("own_z", 1, 0)
             self.to("z_s", 1, 0, "sib")
 
         def pass_z(self):
-            self.to("z_r", 1, 0, "xr")
-            self.to("z_l", 1, 0, "xl")
+            if self.mode != "C":
+                part = 0 if self.mode == "H" else None
+                self.to("z_r", 1, 0, "xr", part)
+                self.to("z_l", 1, 0, "xl", part)
 
         def far(self):
             self.recv("own_rr", 0, 2, 0)
             self.recv("own_ll", 0, 2, 1)
-            self.to("f_z", 0, 2, "zp")
+            if self.mode != "A":
+                self.to("f_z", 0, 2, "zp")
             self.to("f_s", 0, 2, "sib")
 
         def far_z(self):
-            self.recv("f_z", 1, 2)
+            if self.mode == "A":
+                self.recv("z_rr", 1, 2, 0)
+                self.recv("z_ll", 1, 2, 1)
+            else:
+                self.recv("f_z", 1, 2)
             self.to("zf_s", 1, 2, "sib")
 
         def mid(self):
-            self.recv("z_r", 1, -1)
-            self.to("zl_s", 1, -1, "sib")
-            self.recv("z_l", 1, 1)
-            self.to("zr_s", 1, 1, "sib")
+            part = 0 if self.mode == "H" else None
+            if self.mode != "C":
+                self.recv("z_r", 1, -1, part)
+                if self.mode == "A":
+                    self.to("z_rr", 1, -1, "xr", 0)
+                self.recv("z_l", 1, 1, part)
+                if self.mode == "A":
+                    self.to("z_ll", 1, 1, "xl", 1)
+            if self.mode == "C":
+                recv(self.tag + "lr_z", self.pair(6, core))
+            if self.mode == "H":
+                recv(self.tag + "lr_z", self.pair(6, core, 1))
+            self.both("zlr_s", 6)
+
+        def pair(self, i, c, part=None):
+            view = self.buf.at[(slice(i, i + 2), *self.index(c))]
+            return view if part is None else view.at[:, part]
+
+        def both(self, name, i):
+            send(self.tag + name, self.pair(i, core), self.pair(i, core), "sib")
 
         def from_sib(self, i):
-            name = ["own_s", "l_s", "r_s", "z_s", "f_s", "zf_s", "zl_s", "zr_s"][i]
-            self.recv(name, *ORDER[i], None, 1 - core)
+            name = ["own_s", "lr_s", "lr_s", "z_s", "f_s", "zf_s", "zlr_s", "zlr_s"][i]
+            if name in self.seen:
+                return
+            self.seen.add(name)
+            if name in ("lr_s", "zlr_s"):
+                recv(self.tag + name, self.pair(i // 5 * 5 + 1, 1 - core))
+            else:
+                self.recv(name, *ORDER[i], None, 1 - core)
 
     q0, qr, ql, q2 = y * Q, ((y + 1) % 4) * Q, ((y + 3) % 4) * Q, ((y + 2) % 4) * Q
     nt = (((1,), (1,)), ((), ()))
@@ -237,7 +268,7 @@
         for n in range(K // 256):
             cols = slice(n * 256, n * 256 + 256)
             u = jnp.dot(g[s], wc[s, :, :, :, :, :, cols].reshape(S_ROWS, 256), preferred_element_type=F32)
-            u += ua[:, cols] if s != 1 else A * x_ref[:, cols].astype(F32)
+            u += ua[:, cols] if s != 0 else A * x_ref[:, cols].astype(F32)
             if s != 5:
                 ua[:, cols] = u
             else:
@@ -269,130 +300,125 @@
 
     gx[0].own()
     gx[1].own()
-    each(begin, [(0, 1), (0, 0)])
+    each(begin, [(0, 0), (0, 1)])
+    gx[0].near()
+    each(rs2, [(0, 1)])
+    each(begin, [(1, 0)])
     each(rs2, [(0, 0)])
-    gx[0].near()
+    each(begin, [(2, 0)])
+    each(rs3, [(0, 1)])
+    each(rs2, [(1, 0)])
     gx[0].near_z()
-    each(begin, [(2, 0), (1, 0)])
-    each(rs2, [(0, 1)])
+    each(begin, [(3, 0)])
+    gx[1].near_z()
     each(rs3, [(0, 0)])
-    each(rs2, [(1, 0)])
-    each(begin, [(3, 0)])
-    each(rs3, [(0, 1)])
+    gx[1].near()
+    gx[0].pass_z()
     each(rs2, [(2, 0)])
-    gx[1].near()
-    each(begin, [(1, 1)])
     each(rs3, [(1, 0)])
-    gx[1].near_z()
     each(rs2, [(3, 0)])
-    each(begin, [(2, 1)])
     gx[0].far()
-    each(begin, [(3, 1)])
-    each(rs4, [(0, 0)])
-    gx[0].pass_z()
+    each(begin, [(1, 1), (3, 1), (2, 1)])
+    gx[1].pass_z()
+    each(begin, [(4, 0)])
     each(rs2, [(1, 1)])
-    each(begin, [(4, 0)])
-    each(rs2, [(3, 1)])
+    each(rs4, [(0, 1)])
     gx[1].far()
     each(begin, [(4, 1)])
-    each(rs3, [(1, 1)])
-    each(rs4, [(0, 1)])
-    each(rs2, [(4, 0), (2, 1)])
-    each(rs3, [(3, 0)])
-    each(rs2, [(4, 1)])
-    gx[1].pass_z()
+    each(rs2, [(2, 1), (3, 1), (4, 0), (4, 1)])
     gx[0].far_z()
     gx[0].mid()
-    each(begin, [(7, 0), (6, 0)])
-    each(rs3, [(2, 1)])
-    each(begin, [(5, 0)])
-    each(rs2, [(7, 0), (5, 0)])
-    each(rs3, [(2, 0)])
-    each(rs2, [(6, 0)])
+    each(begin, [(5, 0), (6, 0)])
+    each(rs3, [(1, 1), (4, 1), (3, 1)])
+    each(begin, [(7, 0)])
+    each(rs2, [(5, 0), (6, 0), (7, 0)])
     gx[1].far_z()
+    each(rs3, [(2, 1), (2, 0)])
+    each(begin, [(5, 1)])
+    each(rs4, [(1, 0), (4, 1)])
+    each(rs3, [(3, 0)])
+    each(rs4, [(1, 1), (0, 0)])
     gx[1].mid()
-    each(rs4, [(1, 0), (1, 1)])
     each(rs3, [(4, 0)])
-    each(begin, [(5, 1)])
-    each(rs3, [(3, 1)])
+    gg[0].own(0)
+    each(rs3, [(5, 0)])
+    each(begin, [(7, 1)])
+    each(rs4, [(2, 1)])
+    each(rs3, [(7, 0)])
+    product(*w0, 0, 2)
+    each(rs4, [(3, 1)])
     each(begin, [(6, 1)])
-    gg[0].own(0)
-    each(begin, [(7, 1)])
-    each(rs4, [(2, 0), (2, 1)])
-    each(rs3, [(4, 1), (5, 0)])
-    each(rs2, [(5, 1), (6, 1)])
-    product(*w0, 0, 2)
+    each(rs2, [(5, 1)])
+    each(rs3, [(6, 0)])
+    each(rs4, [(3, 0)])
     each(rs2, [(7, 1)])
-    each(rs3, [(7, 0)])
-    each(rs4, [(4, 0), (3, 1)])
+    each(rs4, [(2, 0)])
+    each(rs2, [(6, 1)])
+    each(rs4, [(4, 0)])
     each(rs3, [(5, 1)])
-    each(rs4, [(3, 0)])
+    gg[1].own(0)
+    each(rs3, [(7, 1)])
+    each(rs4, [(7, 0)])
     gg[0].own(1)
     each(rs3, [(6, 1)])
-    each(rs4, [(4, 1)])
+    product(*w0, 2, 5)
+    each(rs4, [(6, 0), (7, 1), (5, 0), (5, 1), (6, 1)])
+    product(*w0, 5, 8)
+    gg[2].own(0)
+    gw[0].own()
     gg[1].own(1)
-    gg[1].own(0)
-    each(rs4, [(5, 0)])
-    each(rs3, [(7, 1)])
-    product(*w0, 2, 5)
-    each(rs4, [(6, 1), (7, 0)])
-    each(rs3, [(6, 0)])
-    each(rs4, [(7, 1), (5, 1), (6, 0)])
-    gg[2].own(0)
     gg[2].own(1)
-    product(*w0, 5, 8)
-    gw[0].own()
     gg[0].near(0)
     gg[0].near(1)
+    product(*w1, 0, 2)
+    gw[0].near()
+    gg[1].near(0)
+    gg[2].near(0)
+    product(*w1, 2, 8)
+    gw[1].own()
+    product(*w2, 0, 2)
     gg[1].near(1)
-    product(*w2, 0, 5)
-    gw[0].near()
-    product(*w1, 0, 2)
     gw[0].near_z()
-    gg[1].near(0)
-    product(*w1, 2, 5)
     gw[0].pass_z()
-    gg[2].near(0)
-    product(*w1, 5, 8)
-    gw[1].own()
-    gw[0].mid()
+    product(*w2, 2, 5)
+    gw[0].far()
+    gw[1].near_z()
     gg[2].near(1)
     product(*w2, 5, 8)
     gw[2].own()
-    gw[0].far()
+    gw[1].pass_z()
+    gg[0].far()
     gw[1].near()
-    gg[0].far()
+    gw[2].near()
+    gw[2].near_z()
+    gw[2].pass_z()
     product(*w3, 0, 2)
-    gw[1].near_z()
-    gw[1].pass_z()
     gg[1].far()
     product(*w3, 2, 5)
-    gw[2].near_z()
-    gw[2].near()
-    gw[1].far()
     gg[2].far()
     product(*w3, 5, 8)
     gw[3].own()
-    gw[2].far()
-    gw[1].far_z()
-    gw[2].pass_z()
-    gw[0].far_z()
-    gw[3].near()
+    gw[0].mid()
+    end(0)
+    gw[1].far()
     gw[3].near_z()
     gw[3].pass_z()
+    gw[3].near()
+    gw[0].far_z()
+    end(3)
+    gw[2].mid()
     end(1)
-    end(0)
+    gw[2].far()
+    gw[1].mid()
+    gw[1].far_z()
     end(2)
+    gw[3].mid()
+    end(7)
     gw[3].far()
+    end(6)
     gw[2].far_z()
-    gw[1].mid()
-    end(3)
+    gw[3].far_z()
     end(4)
-    gw[2].mid()
-    gw[3].mid()
-    end(6)
-    gw[3].far_z()
-    end(7)
     end(5)
 
     for copy in pending[-N_SEND:]:

time: 130 us -> 126 us (0.969)
  Pallas kernels: 128 us -> 124 us
    pallas_call x1, Pallas kernels: 128 us -> 124 us  [shards(): pl.pallas_call(kernel, out_shape=jax.ShapeDtypeStruct((R, K), BF), in_spe...]
where the time goes in v4:
time: 126 us
  Pallas kernels  124 us (98%)
  local copies, waits for them, and re-layouts  2.06 us (2%)
    pallas_call x1, Pallas kernels, shards(): pl.pallas_call(kernel, out_shape=jax.ShapeDtypeStruct((R, K), BF), in_spe...  124 us

profile of v4, /device:TPU:1, one launch (start us, length us, event | category | flops | bytes accessed | tf_op | source)
XLA Modules:
  0.0 126.1 jit_solution(6927295948468922447)
XLA Ops:
  0.0 124.0 %shard_map.17 = bf16[384,1024]{1,0:T(8,128)(2,1)} custom-call(bf16[384,1024]{1,0:T(8,128)(2,1)} %x_hbm.1), custom_call_target="tpu_custom_call" | custom-call | flops 15000000512 | bytes 1572864 | tf_op jit(solution)/shard_map/pallas_call | solution.py:431
  124.1 2.1 %copy.3 = bf16[384,1024]{1,0:T(8,128)(2,1)} copy(bf16[384,1024]{1,0:T(8,128)(2,1)} %shard_map.17) | data formatting | bytes 1572864

commit v5 on v4

--- a/solution.py
+++ b/solution.py
@@ -26,7 +26,7 @@
 ORDER = [(0, 0), (0, 3), (0, 1), (1, 0), (0, 2), (1, 2), (1, 3), (1, 1)]
 SHAPE = (8, 2, 2, 2, 2, H, K)
 HALF = R
-N_SEND = 56
+N_SEND = 40
 N_RECV = 182
 MODES = {"x0": "B", "x1": "B", "w0": "B", "w1": "C", "w2": "B", "w3": "A"}
 GROUPS = [(0, 2), (2, 5), (5, 8)]
@@ -323,19 +323,21 @@
     each(begin, [(4, 0)])
     each(rs2, [(1, 1)])
     each(rs4, [(0, 1)])
+    each(rs2, [(3, 1)])
     gx[1].far()
     each(begin, [(4, 1)])
-    each(rs2, [(2, 1), (3, 1), (4, 0), (4, 1)])
+    each(rs2, [(2, 1), (4, 0), (4, 1)])
     gx[0].far_z()
     gx[0].mid()
     each(begin, [(5, 0), (6, 0)])
     each(rs3, [(1, 1), (4, 1), (3, 1)])
+    each(rs4, [(1, 0)])
     each(begin, [(7, 0)])
     each(rs2, [(5, 0), (6, 0), (7, 0)])
     gx[1].far_z()
     each(rs3, [(2, 1), (2, 0)])
     each(begin, [(5, 1)])
-    each(rs4, [(1, 0), (4, 1)])
+    each(rs4, [(4, 1)])
     each(rs3, [(3, 0)])
     each(rs4, [(1, 1), (0, 0)])
     gx[1].mid()
@@ -343,17 +345,15 @@
     gg[0].own(0)
     each(rs3, [(5, 0)])
     each(begin, [(7, 1)])
-    each(rs4, [(2, 1)])
+    each(rs4, [(2, 1), (3, 1)])
     each(rs3, [(7, 0)])
     product(*w0, 0, 2)
-    each(rs4, [(3, 1)])
     each(begin, [(6, 1)])
     each(rs2, [(5, 1)])
+    each(rs4, [(2, 0)])
     each(rs3, [(6, 0)])
     each(rs4, [(3, 0)])
-    each(rs2, [(7, 1)])
-    each(rs4, [(2, 0)])
-    each(rs2, [(6, 1)])
+    each(rs2, [(7, 1), (6, 1)])
     each(rs4, [(4, 0)])
     each(rs3, [(5, 1)])
     gg[1].own(0)
@@ -386,8 +386,8 @@
     gg[2].near(1)
     product(*w2, 5, 8)
     gw[2].own()
+    gg[0].far()
     gw[1].pass_z()
-    gg[0].far()
     gw[1].near()
     gw[2].near()
     gw[2].near_z()

time: 126 us -> 126 us (level)
  no operation moved by 1% of the time
where the time goes in v5:
time: 126 us; the launch traced here: 125 us
  Pallas kernels  123 us (98%)
  local copies, waits for them, and re-layouts  2.06 us (2%)
    pallas_call x1, Pallas kernels, shards(): pl.pallas_call(kernel, out_shape=jax.ShapeDtypeStruct((R, K), BF), in_spe...  123 us

profile of v5, /device:TPU:1, one launch (start us, length us, event | category | flops | bytes accessed | tf_op | source)
XLA Modules:
  0.0 125.4 jit_solution(14699531971296247620)
XLA Ops:
  0.0 123.3 %shard_map.17 = bf16[384,1024]{1,0:T(8,128)(2,1)} custom-call(bf16[384,1024]{1,0:T(8,128)(2,1)} %x_hbm.1), custom_call_target="tpu_custom_call" | custom-call | flops 15000000512 | bytes 1572864 | tf_op jit(solution)/shard_map/pallas_call | solution.py:431
  123.3 2.1 %copy.3 = bf16[384,1024]{1,0:T(8,128)(2,1)} copy(bf16[384,1024]{1,0:T(8,128)(2,1)} %shard_map.17) | data formatting | bytes 1572864
